TPU v7x, 32 devices: a whole 2x2x4 slice. The times are simulated.
32 devices in a mesh: tm: 16 (over z, y, core), head: 2 (over x).
Axes of the slice: x: 2, y: 2, z: 4, core: 2. Of those that a mesh axis runs over, the one named last changes fastest.
Arguments:
- frames: bfloat16 [8192, 1024], P('tm'), may hold values from -8 to 8
- norm_gain: float32 [1024], replicated, may hold values from 0.5 to 1.5
- w_qkv: bfloat16 [3, 1024, 1024], P(None, 'tm', 'head'), may hold values from -6 to 6
- slopes: float32 [8], P('head'), may hold values from 3.0517578e-05 to 0.05
- w_out: bfloat16 [1024, 1024], P('head', 'tm'), may hold values from -0.5 to 0.5
Outputs:
- attended: bfloat16 [8192, 1024], P(('tm', 'head'))
All inputs are finite; a program needn't handle non-finite values.
Results may differ from a plain program's by a relative error of at most 0.014.
Values may be sent and summed in bfloat16 or wider, within the bound.
A program may use at most 192 MiB of HBM per device.

v0:
```python
import jax
import jax.numpy as jnp
from jax import lax
from jax.sharding import PartitionSpec as P


def local(frames, norm_gain, w_qkv, slopes, w_out):
    frame_count = frames.shape[0]
    local_heads = slopes.shape[0]
    head_size = w_qkv.shape[2] // local_heads
    tm_count = lax.axis_size("tm")
    clip_len = frame_count * tm_count
    me_tm = lax.axis_index("tm")
    scale = head_size ** (-0.5)
    wide = frames.astype(jnp.float32)
    mean_square = jnp.mean(wide * wide, axis=-1, keepdims=True)
    inverse_root = lax.rsqrt(mean_square + 1e-06)
    normed = (wide * inverse_root * norm_gain).astype(jnp.bfloat16)
    projected = jnp.einsum(
        "rd,cde->cre",
        normed,
        lax.all_gather(w_qkv, "tm", axis=1, tiled=True),
        preferred_element_type=jnp.float32,
    ).astype(jnp.bfloat16)
    query = projected[0].reshape(frame_count, local_heads, head_size)
    keyed = projected[1].reshape(frame_count, local_heads, head_size)
    valued = projected[2].reshape(frame_count, local_heads, head_size)
    row_pos = me_tm * frame_count + jnp.arange(frame_count, dtype=jnp.int32)
    key_piece = lax.all_gather(keyed, "tm", axis=0, tiled=True)
    peak = jnp.full((local_heads, frame_count), -1e30, jnp.float32)
    scores = (
        jnp.einsum("qhd,khd->hqk", query, key_piece, preferred_element_type=jnp.float32) * scale
    )
    key_pos = jnp.arange(key_piece.shape[0], dtype=jnp.int32)
    differ = (key_pos[None, :] - row_pos[:, None]) % clip_len
    distance = jnp.minimum(differ, clip_len - differ).astype(jnp.float32)
    scores = scores - slopes[:, None, None] * distance[None, :, :]
    new_peak = jnp.maximum(peak, jnp.max(scores, axis=-1))
    expo = jnp.exp(scores - new_peak[:, :, None])
    totals = jnp.sum(expo, axis=-1)
    accum = jnp.einsum(
        "hqk,khd->hqd",
        expo.astype(jnp.bfloat16),
        lax.all_gather(valued, "tm", axis=0, tiled=True),
        preferred_element_type=jnp.float32,
    )
    state = (new_peak, totals, accum)
    peak, totals, accum = state
    mixed = (accum / totals[:, :, None]).astype(jnp.bfloat16)
    mixed = jnp.transpose(mixed, (1, 0, 2)).reshape(frame_count, local_heads * head_size)
    out_local = lax.all_gather(w_out, "tm", axis=1, tiled=True)
    return lax.psum_scatter(
        jnp.dot(mixed, out_local, preferred_element_type=jnp.float32).astype(jnp.bfloat16),
        "head",
        scatter_dimension=0,
        tiled=True,
    )


def solution(mesh):
    in_specs = (P("tm", None), P(), P(None, "tm", "head"), P("head"), P("head", "tm"))
    out_specs = P(("tm", "head"), None)
    return jax.shard_map(local, mesh=mesh, in_specs=in_specs, out_specs=out_specs, check_vma=False)
```

profile of v0, /device:TPU:0, one launch (start us, length us, event | category | flops | bytes accessed | tf_op | source)
XLA Modules:
  0.0 283.2 jit_solution(9699334613824104066)
XLA Ops:
  6.5 0.0 all-gather.5.cloned.1.call-start
  6.5 0.7 all-gather.5.cloned.1.call-update
  7.3 0.0 copy-start
  7.3 0.0 all-gather.7.cloned.1.call-start
  7.3 1.5 fusion.10
  8.8 48.7 %all-gather.5.cloned.1.call-done = bf16[3,1024,512]{2,1,0:T(8,128)(2,1)} async-done(((bf16[3,64,512]{2,1,0:T(8,128)(2,1)}), bf16[3,1024,512]{2,1,0:T(8,128)(2,1)}) %all-gather.5.cloned.1.call-update) | async-done | bytes 3145744 | tf_op jit(solution)/shard_map/all_gather | solution.py:22
  57.5 4.2 %fusion.13 = bf16[3,512,512]{1,2,0:T(8,128)(2,1)S(1)} fusion(bf16[3,1024,512]{2,1,0:T(8,128)(2,1)} %all-gather.5.cloned.1.call-done, bf16[512,1024]{1,0:T(8,128)(2,1)} %param.5, f32[1024]{0:T(1024)} %param.6, f32[512]{0:T(512)S(1)} %add_rsqrt_fusion), kind=kOutput, calls=%fused_computation.21 | convolution fusion | flops 1613496320 | bytes 5773312 | tf_op jit(solution)/shard_map/rd,cde->cre/dot_general | solution.py:19
  61.7 0.9 fusion.28
  62.6 1.0 copy.6
  63.6 0.0 all-gather.7.cloned.1.call-update
  63.6 0.0 all-gather.9.cloned.1.call-start
  63.7 0.7 all-gather.9.cloned.1.call-update
  64.3 0.0 all-gather.11.cloned.1.call-start
  64.4 0.5 all-gather.11.cloned.1.call-update
  64.9 0.2 reduce-scatter.2.cloned.1.call-start
  65.2 11.0 %fusion.6 = f32[512,8192]{1,0:T(8,128)} fusion(s32[512]{0:T(512)S(1)} %iota_add_fusion), kind=kLoop, calls=%fused_computation.11 | loop fusion | flops 62914560 | bytes 16779264 | tf_op jit(solution)/shard_map/convert_element_type | solution.py:36
  76.1 61.4 %all-gather.7.cloned.1.call-done = bf16[8192,4,128]{2,0,1:T(8,128)(2,1)} async-done(((bf16[512,4,128]{2,0,1:T(8,128)(2,1)}), bf16[8192,4,128]{2,0,1:T(8,128)(2,1)}) %all-gather.7.cloned.1.call-update) | async-done | bytes 8388624 | tf_op jit(solution)/shard_map/all_gather | solution.py:29
  137.5 0.0 copy-done
  137.5 33.0 %fusion.2 = (f32[4,512]{1,0:T(4,128)S(1)}, f32[4,512,8192]{2,1,0:T(8,128)}) fusion(f32[512,8192]{1,0:T(8,128)} %fusion.6, f32[4]{0:T(128)S(1)} %copy-done, bf16[512,4,128]{0,2,1:T(8,128)(2,1)S(1)} %bitcast.22, bf16[8192,4,128]{2,0,1:T(8,128)(2,1)} %all-gather.7.cloned.1.call-done), kind=kOutput, calls=%fused_computation.4 | convolution fusion | flops 4362074112 | bytes 92807184 | tf_op jit(solution)/shard_map/qhd,khd->hqk/dot_general | solution.py:32
  170.5 32.8 %fusion = f32[4,512]{1,0:T(4,128)S(1)} fusion(f32[4,512,8192]{2,1,0:T(8,128)} %get-tuple-element.9, f32[4,512]{1,0:T(4,128)S(1)} %broadcast_maximum_fusion, f32[512,8192]{1,0:T(8,128)} %fusion.6, f32[4]{0:T(128)S(1)} %copy-done), kind=kLoop, calls=%fused_computation.2 | loop fusion | flops 83884032 | bytes 83902480 | tf_op jit(solution)/shard_map/reduce_sum | solution.py:40
  203.3 12.7 %all-gather.9.cloned.1.call-done = bf16[8192,4,128]{0,2,1:T(8,128)(2,1)} async-done(((bf16[512,4,128]{0,2,1:T(8,128)(2,1)}), bf16[8192,4,128]{0,2,1:T(8,128)(2,1)}) %all-gather.9.cloned.1.call-update) | async-done | bytes 8388624 | tf_op jit(solution)/shard_map/all_gather | solution.py:44
  216.0 31.4 %fusion.20 = bf16[512,4,128]{0,2,1:T(8,128)(2,1)S(1)} fusion(bf16[8192,4,128]{0,2,1:T(8,128)(2,1)} %all-gather.9.cloned.1.call-done, f32[4,512,8192]{2,1,0:T(8,128)} %get-tuple-element.9, f32[4,512]{1,0:T(4,128)S(1)} %broadcast_maximum_fusion, f32[512,8192]{1,0:T(8,128)} %fusion.6, f32[4]{0:T(128)S(1)} %copy-done, f32[512,4]{0,1:T(4,128)S(1)} %bitcast.26), kind=kOutput, calls=%fused_computation.25 | convolution fusion | flops 4379377664 | bytes 92815376 | tf_op jit(solution)/shard_map/hqk,khd->hqd/dot_general | solution.py:41
  247.4 6.8 %all-gather.11.cloned.1.call-done = bf16[512,1024]{0,1:T(8,128)(2,1)} async-done(((bf16[512,64]{0,1:T(8,128)(2,1)}), bf16[512,1024]{0,1:T(8,128)(2,1)}) %all-gather.11.cloned.1.call-update) | async-done | bytes 1048592 | tf_op jit(solution)/shard_map/all_gather | solution.py:51
  254.2 3.0 %convolution_convert_fusion.1 = bf16[512,1024]{1,0:T(8,128)(2,1)} fusion(bf16[512,512]{0,1:T(8,128)(2,1)S(1)} %bitcast.25, bf16[512,1024]{0,1:T(8,128)(2,1)} %all-gather.11.cloned.1.call-done), kind=kOutput, calls=%fused_computation.22 | convolution fusion | flops 537395200 | bytes 2621440 | tf_op jit(solution)/shard_map/dot_general | solution.py:53
  257.2 0.0 reduce-scatter.2.cloned.1.call-update
  257.2 19.4 %reduce-scatter.2.cloned.1.call-done = bf16[256,1024]{1,0:T(8,128)(2,1)} async-done(((bf16[512,1024]{1,0:T(8,128)(2,1)}), bf16[256,1024]{1,0:T(8,128)(2,1)}) %reduce-scatter.2.cloned.1.call-update) | async-done | bytes 524304 | tf_op jit(solution)/shard_map/reduce_scatter | solution.py:52
  (3 shorter events, 0.0 us)
Async XLA Ops:
  6.5 51.0 %all-gather.5.cloned.1.call-start = ((), (), s32[]{:S(2)}) async-start(), calls=%async_computation.1 | async-start | bytes 3342336 | tf_op jit(solution)/shard_map/all_gather | solution.py:22
  7.3 130.2 %copy-start = (f32[4]{0:T(128)S(1)}, f32[4]{0:T(128)}, u32[]{:S(2)}) copy-start(f32[4]{0:T(128)} %param.8) | copy-start | bytes 52
  7.3 130.2 %all-gather.7.cloned.1.call-start = ((), (), s32[]{:S(2)}) async-start(), calls=%async_computation.2 | async-start | bytes 8912896 | tf_op jit(solution)/shard_map/all_gather | solution.py:29
  63.6 152.4 %all-gather.9.cloned.1.call-start = ((), (), s32[]{:S(2)}) async-start(), calls=%async_computation.3 | async-start | bytes 8912896 | tf_op jit(solution)/shard_map/all_gather | solution.py:44
  64.3 189.9 %all-gather.11.cloned.1.call-start = ((), (), s32[]{:S(2)}) async-start(), calls=%async_computation.4 | async-start | bytes 1114112 | tf_op jit(solution)/shard_map/all_gather | solution.py:51
  64.9 211.7 %reduce-scatter.2.cloned.1.call-start = ((), (), s32[]{:S(2)}) async-start(), calls=%async_computation.5 | async-start | bytes 1572864 | tf_op jit(solution)/shard_map/reduce_scatter | solution.py:52
Sparse Core Ops, SparseCore 0:
  9.5 47.9 all-gather.4
  63.7 73.7 all-gather.6
  139.7 76.3 all-gather.8
  218.0 36.1 all-gather.10
  257.3 19.2 reduce-scatter.1
where the time goes:
time: 283 us
  waiting for transfers between devices  151 us (53%)
  matrix products  71.5 us (25%)
  other arithmetic  45.3 us (16%)
  between operations  13.2 us (5%)
    all_gather x1, waiting for transfers between devices, local(): key_piece = lax.all_gather(keyed, 'tm', axis=0, tiled=True)  61.4 us
    all_gather x1, waiting for transfers between devices, local(): lax.all_gather(w_qkv, 'tm', axis=1, tiled=True)  48.7 us
    dot_general x1, matrix products, local(): jnp.einsum('qhd,khd->hqk', query, key_piece, preferred_element_type=jnp.f...  33 us
    reduce_sum x1, other arithmetic, local(): totals = jnp.sum(expo, axis=-1)  32.8 us
    dot_general x1, matrix products, local(): jnp.einsum('hqk,khd->hqd', expo.astype(jnp.bfloat16), lax.all_gather(valu...  31.4 us
    reduce_scatter x1, waiting for transfers between devices, local(): lax.psum_scatter(jnp.dot(mixed, out_local, preferred_element_type=jnp.flo...  19.4 us
    all_gather x1, waiting for transfers between devices, local(): lax.all_gather(valued, 'tm', axis=0, tiled=True)  12.7 us
    convert_element_type x1, other arithmetic, local(): distance = jnp.minimum(differ, clip_len - differ).astype(jnp.float32)  11 us
  transfers between devices with their start and end apart: 5, of which 5 were waited for; matrix products, arithmetic and copies ran while one was open for 39% of the time, Pallas kernels for 0%

commit v1 on v0

v1 whole, which is shorter than its diff:
```python
import functools
import math
import jax
import jax.numpy as jnp
from jax import lax
from jax.experimental import pallas as pl
from jax.experimental.pallas import tpu as pltpu
from jax.sharding import PartitionSpec as P

MESH = pl.DeviceIdType.MESH
ZS = 4
F32 = jnp.float32
BF16 = jnp.bfloat16


def flip(z, d):
    lo, hi = z % 2, z // 2
    dlo, dhi = d % 2, d // 2
    return (lo + dlo) % 2 + 2 * ((hi + dhi) % 2)


def kernel(
    frames, gain, w, slopes, mixed,
    wbuf, kvbuf, qbuf, kvs, qs, obuf, ost, normed, tiles, acc, peak,
    wz_s, wz_r, wy_s, wy_r, wc_s, wc_r,
    kz_s, kz_r, ky_s, ky_r, kc_s, kc_r,
    qz_s, qz_r, o_s, o_r, l_s,
):
    rows, width = frames.shape
    hd = kvbuf.shape[-1]
    half = rows // 2
    blocks = kvbuf.shape[0]
    tm = lax.axis_index("tm")
    x = lax.axis_index("head")
    z, y, c = tm // 4, (tm // 2) % 2, tm % 2

    def at(zz, yy, cc):
        return zz * 4 + yy * 2 + cc

    def to(index, other=None):
        return (index, x if other is None else other)

    y_peer, c_peer = at(z, 1 - y, c), at(z, y, 1 - c)

    def send(src, dst, ss, rs, dev):
        return pltpu.make_async_remote_copy(
            src_ref=src, dst_ref=dst, send_sem=ss, recv_sem=rs, device_id=dev, device_id_type=MESH
        )

    def w_z(d):
        return send(w, wbuf.at[tm], wz_s.at[d], wz_r.at[d], to(at(flip(z, d), y, c)))

    def w_y(d):
        s = at(flip(z, d), y, c)
        return send(wbuf.at[s], wbuf.at[s], wy_s.at[d], wy_r.at[d], to(y_peer))

    def w_c(d, k):
        s = at(flip(z, d), y if k == 0 else 1 - y, c)
        return send(wbuf.at[s], wbuf.at[s], wc_s.at[d, k], wc_r.at[d, k], to(c_peer))

    def kv_z(d):
        t = flip(z, d)
        return send(kvs.at[t], kvbuf.at[tm], kz_s.at[d], kz_r.at[d], to(at(t, y, c)))

    def kv_y(d):
        s = at(flip(z, d), y, c)
        return send(kvbuf.at[s], kvbuf.at[s], ky_s.at[d], ky_r.at[d], to(y_peer))

    def kv_c(d, k):
        s = at(flip(z, d), y if k == 0 else 1 - y, c)
        return send(kvbuf.at[s], kvbuf.at[s], kc_s.at[d, k], kc_r.at[d, k], to(c_peer))

    def q_z(d):
        t = flip(z, d)
        return send(qs.at[t], qbuf.at[z], qz_s.at[d], qz_r.at[d], to(at(t, y, c)))

    def o_copy(d, k):
        t = flip(z, d)
        xx = x if k == 0 else 1 - x
        return send(
            ost.at[t, xx], obuf.at[x * ZS + z], o_s.at[d, k], o_r.at[d, k], to(at(t, y, c), xx)
        )

    partners = [to(at(flip(z, d), y, c)) for d in (1, 2, 3)] + [to(y_peer), to(c_peer)]
    partners += [to(at(flip(z, d), y, c), 1 - x) for d in range(4)]
    barrier = pltpu.get_barrier_semaphore()
    for dev in partners:
        pl.semaphore_signal(barrier, inc=1, device_id=dev, device_id_type=MESH)
    pl.semaphore_wait(barrier, len(partners))

    for d in (1, 2, 3):
        w_z(d).start()
    wbuf[tm] = w[...]
    w_y(0).start()
    w_c(0, 0).start()

    wide = frames[...].astype(F32)
    inverse_root = lax.rsqrt(jnp.mean(wide * wide, axis=-1, keepdims=True) + 1e-06)
    normed[...] = (wide * inverse_root * gain[...]).astype(BF16)

    log2e = math.log2(math.e)
    slope = slopes[z] * log2e
    ii = lax.broadcasted_iota(jnp.int32, (rows, rows), 0)
    jj = lax.broadcasted_iota(jnp.int32, (rows, rows), 1)
    lin = (ii - jj).astype(F32) * slope
    tiles[0] = -jnp.abs(lin)
    tiles[1] = -lin
    tiles[2] = jnp.abs(lin)
    tiles[3] = lin
    acc[...] = jnp.zeros_like(acc)
    peak[...] = jnp.full_like(peak, -1e30)

    for d in (1, 2, 3):
        w_z(d).wait_recv()
        w_y(d).start()
        w_c(d, 0).start()
    for d in range(4):
        w_y(d).wait_recv()
        w_c(d, 1).start()
    for d in range(4):
        w_c(d, 0).wait_recv()
        w_c(d, 1).wait_recv()

    def project(part):
        weights = wbuf[:, part].reshape(width, ZS * hd)
        return jnp.dot(normed[...], weights, preferred_element_type=F32)

    for part in (1, 2):
        res = project(part).astype(BF16)
        for h in range(ZS):
            kvs[h, part - 1] = res[:, h * hd:(h + 1) * hd]
    for d in (1, 2, 3):
        kv_z(d).start()
    kvbuf[tm] = kvs[z]
    kv_y(0).start()
    kv_c(0, 0).start()
    res = (project(0) * (hd ** -0.5 * log2e)).astype(BF16)
    for h in range(ZS):
        qs[h] = res[:, h * hd:(h + 1) * hd]
    for d in (1, 2, 3):
        q_z(d).start()
    qbuf[z] = qs[z]
    kv_y(0).wait_recv()
    kv_c(0, 1).start()

    ones = jnp.ones((rows, hd), BF16)

    def step(t, carry):
        d, i = t // 4, t % 4
        zk = flip(z, d)
        e = jnp.where(d == 3, 3 - i, i)
        zq = flip(z, e)

        @pl.when(i == 0)
        def _():
            kv_c(d, 0).wait_recv()
            kv_c(d, 1).wait_recv()

        @pl.when(jnp.logical_and(d == 0, i > 0))
        def _():
            q_z(i).wait_recv()

        @pl.when(jnp.logical_and(d < 3, i == 1))
        def _():
            kv_z(d + 1).wait_recv()
            kv_y(d + 1).start()
            kv_c(d + 1, 0).start()

        @pl.when(jnp.logical_and(d < 3, i == 3))
        def _():
            kv_y(d + 1).wait_recv()
            kv_c(d + 1, 1).start()

        me = at(zq, y, c)
        kinds, bases = [], []
        for k in range(4):
            delta = (me - (zk * 4 + k) + blocks) % blocks
            middle = blocks // 2
            kind = jnp.where(
                delta == 0, 0, jnp.where(delta < middle, 1, jnp.where(delta == middle, 2, 3))
            )
            kinds.append(kind)
            far = jnp.where(delta <= middle, delta, blocks - delta) * rows
            bases.append(-slope * far.astype(F32))
        for r in (0, half):
            q = qbuf[zq, r:r + half, :]
            place = pl.ds(pl.multiple_of(zq * rows + r, half), half)
            raw, top = [], None
            for k in range(4):
                s = lax.dot_general(
                    q, kvbuf[zk * 4 + k, 0], (((1,), (1,)), ((), ())), preferred_element_type=F32
                )
                s = s + tiles[kinds[k], r:r + half, :]
                raw.append(s)
                m = s[:, :hd]
                for a in range(hd, rows, hd):
                    m = jnp.maximum(m, s[:, a:a + hd])
                m = m + bases[k]
                top = m if top is None else jnp.maximum(top, m)
            old = peak[place, :]
            new = jnp.maximum(old, jnp.max(top, axis=-1, keepdims=True))
            peak[place, :] = new
            shrink = jnp.exp2(old - new)
            col = new[:, :1]
            total = acc[place, :] * jnp.concatenate([shrink, shrink], axis=1)
            for k in range(4):
                p = jnp.exp2(raw[k] - (col - bases[k])).astype(BF16)
                v = jnp.concatenate([kvbuf[zk * 4 + k, 1], ones], axis=1)
                total = total + jnp.dot(p, v, preferred_element_type=F32)
            acc[place, :] = total

        @pl.when(d == 3)
        def _():
            for s in range(2):
                place = pl.ds(pl.multiple_of(zq * rows + s * half, half), half)
                val = acc[place, :]
                ost[zq, s] = (val[:, :hd] / val[:, hd:]).astype(BF16)
            o_copy(e, 1).start()

        @pl.when(jnp.logical_and(d == 3, e > 0))
        def _():
            o_copy(e, 0).start()

        return carry

    lax.fori_loop(0, 16, step, 0)

    obuf[x * ZS + z] = ost[z, x]
    for d in range(4):
        o_copy(d, 1).wait_recv()
        if d:
            o_copy(d, 0).wait_recv()
    mixed[...] = obuf[...]

    for d in range(4):
        if d:
            w_z(d).wait_send()
            kv_z(d).wait_send()
            q_z(d).wait_send()
            o_copy(d, 0).wait_send()
        w_y(d).wait_send()
        w_c(d, 0).wait_send()
        w_c(d, 1).wait_send()
        kv_y(d).wait_send()
        kv_c(d, 0).wait_send()
        kv_c(d, 1).wait_send()
        o_copy(d, 1).wait_send()


def local_planes(frames, norm_gain, w_qkv, slopes, w_out):
    rows, width = frames.shape
    blocks = lax.axis_size("tm")
    heads = slopes.shape[0]
    hd = w_qkv.shape[2] // heads
    total = heads * lax.axis_size("head")
    half = rows // 2
    w_all = lax.all_gather(w_out, "tm", axis=1, tiled=True)
    w_all = lax.all_gather(w_all, "head", axis=0, tiled=True)
    dma = pltpu.SemaphoreType.DMA
    vmem = pl.BlockSpec(memory_space=pltpu.VMEM)
    mixed = pl.pallas_call(
        kernel,
        out_shape=jax.ShapeDtypeStruct((total, half, hd), BF16),
        in_specs=[vmem, vmem, vmem, pl.BlockSpec(memory_space=pltpu.SMEM)],
        out_specs=vmem,
        scratch_shapes=[
            pltpu.VMEM((blocks,) + w_qkv.shape, BF16),
            pltpu.VMEM((blocks, 2, rows, hd), BF16),
            pltpu.VMEM((ZS, rows, hd), BF16),
            pltpu.VMEM((ZS, 2, rows, hd), BF16),
            pltpu.VMEM((ZS, rows, hd), BF16),
            pltpu.VMEM((total, half, hd), BF16),
            pltpu.VMEM((ZS, 2, half, hd), BF16),
            pltpu.VMEM((rows, width), BF16),
            pltpu.VMEM((4, rows, rows), F32),
            pltpu.VMEM((ZS * rows, 2 * hd), F32),
            pltpu.VMEM((ZS * rows, hd), F32),
        ] + [
            dma((4,)), dma((4,)), dma((4,)), dma((4,)), dma((4, 2)), dma((4, 2)),
            dma((4,)), dma((4,)), dma((4,)), dma((4,)), dma((4, 2)), dma((4, 2)),
            dma((4,)), dma((4,)), dma((4, 2)), dma((4, 2)), dma((1,)),
        ],
        compiler_params=pltpu.CompilerParams(
            collective_id=0, has_side_effects=True, vmem_limit_bytes=56 * 1024 * 1024
        ),
        cost_estimate=pl.CostEstimate(
            flops=11 * 10 ** 9, bytes_accessed=6 * 10 ** 6, transcendentals=17 * 10 ** 6
        ),
    )(frames, norm_gain.reshape(1, -1), w_qkv, slopes)
    flat = jnp.transpose(mixed, (1, 0, 2)).reshape(half, total * hd)
    return jnp.dot(flat, w_all, preferred_element_type=F32).astype(BF16)


def local(frames, norm_gain, w_qkv, slopes, w_out):
    frame_count = frames.shape[0]
    local_heads = slopes.shape[0]
    head_size = w_qkv.shape[2] // local_heads
    tm_count = lax.axis_size("tm")
    clip_len = frame_count * tm_count
    me_tm = lax.axis_index("tm")
    scale = head_size ** (-0.5)
    wide = frames.astype(F32)
    mean_square = jnp.mean(wide * wide, axis=-1, keepdims=True)
    inverse_root = lax.rsqrt(mean_square + 1e-06)
    normed = (wide * inverse_root * norm_gain).astype(BF16)
    projected = jnp.einsum(
        "rd,cde->cre",
        normed,
        lax.all_gather(w_qkv, "tm", axis=1, tiled=True),
        preferred_element_type=F32,
    ).astype(BF16)
    query, keyed, valued = (
        projected[n].reshape(frame_count, local_heads, head_size) for n in range(3)
    )
    row_pos = me_tm * frame_count + jnp.arange(frame_count, dtype=jnp.int32)
    key_piece = lax.all_gather(keyed, "tm", axis=0, tiled=True)
    scores = jnp.einsum("qhd,khd->hqk", query, key_piece, preferred_element_type=F32) * scale
    key_pos = jnp.arange(key_piece.shape[0], dtype=jnp.int32)
    differ = (key_pos[None, :] - row_pos[:, None]) % clip_len
    distance = jnp.minimum(differ, clip_len - differ).astype(F32)
    scores = scores - slopes[:, None, None] * distance[None, :, :]
    expo = jnp.exp(scores - jnp.max(scores, axis=-1, keepdims=True))
    totals = jnp.sum(expo, axis=-1)
    accum = jnp.einsum(
        "hqk,khd->hqd",
        expo.astype(BF16),
        lax.all_gather(valued, "tm", axis=0, tiled=True),
        preferred_element_type=F32,
    )
    mixed = (accum / totals[:, :, None]).astype(BF16)
    mixed = jnp.transpose(mixed, (1, 0, 2)).reshape(frame_count, local_heads * head_size)
    out_local = lax.all_gather(w_out, "tm", axis=1, tiled=True)
    return lax.psum_scatter(
        jnp.dot(mixed, out_local, preferred_element_type=F32).astype(BF16),
        "head",
        scatter_dimension=0,
        tiled=True,
    )


def solution(mesh):
    in_specs = (P("tm", None), P(), P(None, "tm", "head"), P("head"), P("head", "tm"))
    out_specs = P(("tm", "head"), None)
    planes = mesh.shape["tm"] == 4 * ZS and mesh.shape["head"] == 2
    return jax.shard_map(
        local_planes if planes else local,
        mesh=mesh, in_specs=in_specs, out_specs=out_specs, check_vma=False,
    )
```

time: 283 us -> 170 us (0.60)
  Pallas kernels: 0 us -> 109 us
  waiting for transfers between devices: 151 us -> 43.6 us
  matrix products: 71.5 us -> 3.14 us
  other arithmetic: 45.3 us -> 0 us
    pallas_call x0 -> x1, Pallas kernels: none -> 109 us  [local_planes(): pl.pallas_call(kernel, out_shape=jax.ShapeDtypeStruct((total, half, hd),...]
    all_gather x4 -> x2, waiting for transfers between devices: 130 us -> 42.9 us  [the longest x1 42.9 us: local_planes(): w_all = lax.all_gather(w_out, 'tm', axis=1, tiled=True)]
    dot_general x4 -> x1, matrix products: 71.5 us -> 3.14 us  [local_planes(): return jnp.dot(flat, w_all, preferred_element_type=F32).astype(BF16)]
    reduce_sum x2 -> x0, other arithmetic: 34.3 us -> none  [the longest x1 32.8 us: local(): totals = jnp.sum(expo, axis=-1)]
    reduce_scatter x1 -> x0, waiting for transfers between devices: 19.4 us -> none  [local(): lax.psum_scatter(jnp.dot(mixed, out_local, preferred_element_type=jnp.flo...]
    convert_element_type x1 -> x0, other arithmetic: 11 us -> none  [local(): distance = jnp.minimum(differ, clip_len - differ).astype(jnp.float32)]
  transfers between devices with their start and end apart: 5 -> 2, of which waited for: 5 -> 1; matrix products, arithmetic and copies ran while one was open for 39% -> 1% of each run, Pallas kernels for 0% -> 64%
where the time goes in v1:
time: 170 us
  Pallas kernels  109 us (64%)
  waiting for transfers between devices  43.6 us (26%)
  between operations  13.4 us (8%)
  matrix products  3.14 us (2%)
    pallas_call x1, Pallas kernels, local_planes(): pl.pallas_call(kernel, out_shape=jax.ShapeDtypeStruct((total, half, hd),...  109 us
    all_gather x1, waiting for transfers between devices, local_planes(): w_all = lax.all_gather(w_out, 'tm', axis=1, tiled=True)  42.9 us
  transfers between devices with their start and end apart: 2, of which 1 were waited for; matrix products, arithmetic and copies ran while one was open for 1% of the time, Pallas kernels for 64%

profile of v1, /device:TPU:0, one launch (start us, length us, event | category | flops | bytes accessed | tf_op | source)
XLA Modules:
  0.0 170.2 jit_solution(5304441174884237639)
XLA Ops:
  6.5 0.0 all-gather.3.cloned.1.call-start
  6.5 0.7 all-gather.3.cloned.1.call-update
  7.3 0.0 all-gather.5.cloned.1.call-start
  7.3 42.9 %all-gather.3.cloned.1.call-done = bf16[512,1024]{0,1:T(8,128)(2,1)} async-done(((bf16[512,64]{0,1:T(8,128)(2,1)}), bf16[512,1024]{0,1:T(8,128)(2,1)}) %all-gather.3.cloned.1.call-update) | async-done | bytes 1048592 | tf_op jit(solution)/shard_map/all_gather | solution.py:257
  50.2 0.0 all-gather.5.cloned.1.call-update
  50.2 108.7 %shard_map.55 = bf16[8,256,128]{2,1,0:T(8,128)(2,1)} custom-call(bf16[512,1024]{1,0:T(8,128)(2,1)} %frames.1, f32[1,1024]{1,0:T(1,128)} %bitcast.7, bf16[3,64,512]{2,1,0:T(8,128)(2,1)} %w.1, f32[4]{0:T(128)} %slopes.1), custom_call_target="tpu_custom_call" | custom-call | flops 11000000512 | bytes 6000000 | tf_op jit(solution)/shard_map/pallas_call | solution.py:261
  158.9 1.2 copy.6
  160.1 0.0 all-gather.5.cloned.1.call-done
  160.2 3.1 %convolution_convert_fusion = bf16[256,1024]{1,0:T(8,128)(2,1)} fusion(bf16[256,1024]{0,1:T(8,128)(2,1)S(1)} %bitcast.5, bf16[1024,1024]{0,1:T(8,128)(2,1)} %all-gather.5.cloned.1.call-done), kind=kOutput, calls=%fused_computation | convolution fusion | flops 537133056 | bytes 3145728 | tf_op jit(solution)/shard_map/dot_general | solution.py:291
Async XLA Ops:
  6.5 43.7 %all-gather.3.cloned.1.call-start = ((), (), s32[]{:S(2)}) async-start(), calls=%async_computation | async-start | bytes 1114112 | tf_op jit(solution)/shard_map/all_gather | solution.py:257
  7.3 152.9 %all-gather.5.cloned.1.call-start = ((), (), s32[]{:S(2)}) async-start(), calls=%async_computation.1 | async-start | bytes 3145728 | tf_op jit(solution)/shard_map/all_gather | solution.py:258
Sparse Core Ops, SparseCore 0:
  9.5 40.6 all-gather.2
  51.7 32.0 all-gather.4

commit v2 on v1

--- a/solution.py
+++ b/solution.py
@@ -1,4 +1,3 @@
-import functools
 import math
 import jax
 import jax.numpy as jnp
@@ -20,11 +19,11 @@
 
 
 def kernel(
-    frames, gain, w, slopes, mixed,
-    wbuf, kvbuf, qbuf, kvs, qs, obuf, ost, normed, tiles, acc, peak,
+    frames, gain, w, slopes, w_out, out,
+    wbuf, kvbuf, qbuf, kvs, qs, obuf, ost, normed, tiles, acc, peak, wobuf,
     wz_s, wz_r, wy_s, wy_r, wc_s, wc_r,
     kz_s, kz_r, ky_s, ky_r, kc_s, kc_r,
-    qz_s, qz_r, o_s, o_r, l_s,
+    qz_s, qz_r, o_s, o_r, p_s, p_r,
 ):
     rows, width = frames.shape
     hd = kvbuf.shape[-1]
@@ -37,6 +36,9 @@
     def at(zz, yy, cc):
         return zz * 4 + yy * 2 + cc
 
+    def slot(zz, yy, cc):
+        return zz * 4 + cc * 2 + yy
+
     def to(index, other=None):
         return (index, x if other is None else other)
 
@@ -47,28 +49,30 @@
             src_ref=src, dst_ref=dst, send_sem=ss, recv_sem=rs, device_id=dev, device_id_type=MESH
         )
 
-    def w_z(d):
-        return send(w, wbuf.at[tm], wz_s.at[d], wz_r.at[d], to(at(flip(z, d), y, c)))
-
-    def w_y(d):
-        s = at(flip(z, d), y, c)
-        return send(wbuf.at[s], wbuf.at[s], wy_s.at[d], wy_r.at[d], to(y_peer))
-
-    def w_c(d, k):
-        s = at(flip(z, d), y if k == 0 else 1 - y, c)
-        return send(wbuf.at[s], wbuf.at[s], wc_s.at[d, k], wc_r.at[d, k], to(c_peer))
-
-    def kv_z(d):
+    def w_z(part, d):
+        dev = to(at(flip(z, d), y, c))
+        return send(w.at[part], wbuf.at[part, c, y, z], wz_s.at[part, d], wz_r.at[part, d], dev)
+
+    def w_y(part):
+        ref = wbuf.at[part, c, y]
+        return send(ref, ref, wy_s.at[part], wy_r.at[part], to(y_peer))
+
+    def w_c(part):
+        ref = wbuf.at[part, c]
+        return send(ref, ref, wc_s.at[part], wc_r.at[part], to(c_peer))
+
+    def kv_z(d, j):
         t = flip(z, d)
-        return send(kvs.at[t], kvbuf.at[tm], kz_s.at[d], kz_r.at[d], to(at(t, y, c)))
+        dst = kvbuf.at[slot(z, y, c), j]
+        return send(kvs.at[t, j], dst, kz_s.at[d, j], kz_r.at[d, j], to(at(t, y, c)))
 
     def kv_y(d):
-        s = at(flip(z, d), y, c)
-        return send(kvbuf.at[s], kvbuf.at[s], ky_s.at[d], ky_r.at[d], to(y_peer))
-
-    def kv_c(d, k):
-        s = at(flip(z, d), y if k == 0 else 1 - y, c)
-        return send(kvbuf.at[s], kvbuf.at[s], kc_s.at[d, k], kc_r.at[d, k], to(c_peer))
+        ref = kvbuf.at[slot(flip(z, d), y, c)]
+        return send(ref, ref, ky_s.at[d], ky_r.at[d], to(y_peer))
+
+    def kv_c(d):
+        ref = kvbuf.at[pl.ds(slot(flip(z, d), 0, c), 2)]
+        return send(ref, ref, kc_s.at[d], kc_r.at[d], to(c_peer))
 
     def q_z(d):
         t = flip(z, d)
@@ -81,6 +85,22 @@
             ost.at[t, xx], obuf.at[x * ZS + z], o_s.at[d, k], o_r.at[d, k], to(at(t, y, c), xx)
         )
 
+    def p_z(d):
+        ref = wobuf.at[c, y, x, z]
+        return send(ref, ref, p_s.at[d], p_r.at[d], to(at(flip(z, d), y, c)))
+
+    def p_x():
+        ref = wobuf.at[c, y, x]
+        return send(ref, ref, p_s.at[4], p_r.at[4], to(tm, 1 - x))
+
+    def p_y():
+        ref = wobuf.at[c, y]
+        return send(ref, ref, p_s.at[5], p_r.at[5], to(y_peer))
+
+    def p_c():
+        ref = wobuf.at[c]
+        return send(ref, ref, p_s.at[6], p_r.at[6], to(c_peer))
+
     partners = [to(at(flip(z, d), y, c)) for d in (1, 2, 3)] + [to(y_peer), to(c_peer)]
     partners += [to(at(flip(z, d), y, c), 1 - x) for d in range(4)]
     barrier = pltpu.get_barrier_semaphore()
@@ -88,11 +108,12 @@
         pl.semaphore_signal(barrier, inc=1, device_id=dev, device_id_type=MESH)
     pl.semaphore_wait(barrier, len(partners))
 
-    for d in (1, 2, 3):
-        w_z(d).start()
-    wbuf[tm] = w[...]
-    w_y(0).start()
-    w_c(0, 0).start()
+    for part in range(3):
+        for d in (1, 2, 3):
+            w_z(part, d).start()
+    for part in range(3):
+        wbuf[part, c, y, z] = w[part]
+    wobuf[c, y, x, z] = w_out[...]
 
     wide = frames[...].astype(F32)
     inverse_root = lax.rsqrt(jnp.mean(wide * wide, axis=-1, keepdims=True) + 1e-06)
@@ -100,6 +121,24 @@
 
     log2e = math.log2(math.e)
     slope = slopes[z] * log2e
+
+    def z_arrived(part):
+        for d in (1, 2, 3):
+            w_z(part, d).wait_recv()
+        w_y(part).start()
+
+    def y_arrived(part):
+        w_y(part).wait_recv()
+        w_c(part).start()
+
+    def project(part):
+        w_c(part).wait_recv()
+        weights = jnp.concatenate(
+            [wbuf[part, n % 2, (n // 2) % 2, n // 4] for n in range(blocks)], axis=0
+        )
+        return jnp.dot(normed[...], weights, preferred_element_type=F32)
+
+    z_arrived(0)
     ii = lax.broadcasted_iota(jnp.int32, (rows, rows), 0)
     jj = lax.broadcasted_iota(jnp.int32, (rows, rows), 1)
     lin = (ii - jj).astype(F32) * slope
@@ -109,39 +148,28 @@
     tiles[3] = lin
     acc[...] = jnp.zeros_like(acc)
     peak[...] = jnp.full_like(peak, -1e30)
-
-    for d in (1, 2, 3):
-        w_z(d).wait_recv()
-        w_y(d).start()
-        w_c(d, 0).start()
-    for d in range(4):
-        w_y(d).wait_recv()
-        w_c(d, 1).start()
-    for d in range(4):
-        w_c(d, 0).wait_recv()
-        w_c(d, 1).wait_recv()
-
-    def project(part):
-        weights = wbuf[:, part].reshape(width, ZS * hd)
-        return jnp.dot(normed[...], weights, preferred_element_type=F32)
-
-    for part in (1, 2):
-        res = project(part).astype(BF16)
-        for h in range(ZS):
-            kvs[h, part - 1] = res[:, h * hd:(h + 1) * hd]
-    for d in (1, 2, 3):
-        kv_z(d).start()
-    kvbuf[tm] = kvs[z]
-    kv_y(0).start()
-    kv_c(0, 0).start()
+    z_arrived(1)
+    y_arrived(0)
+    z_arrived(2)
     res = (project(0) * (hd ** -0.5 * log2e)).astype(BF16)
     for h in range(ZS):
         qs[h] = res[:, h * hd:(h + 1) * hd]
     for d in (1, 2, 3):
         q_z(d).start()
     qbuf[z] = qs[z]
+    for part in (1, 2):
+        y_arrived(part)
+        res = project(part).astype(BF16)
+        for h in range(ZS):
+            kvs[h, part - 1] = res[:, h * hd:(h + 1) * hd]
+        for d in (1, 2):
+            kv_z(d, part - 1).start()
+    kvbuf[slot(z, y, c)] = kvs[z]
+    kv_y(0).start()
+    for d in (1, 2, 3):
+        p_z(d).start()
     kv_y(0).wait_recv()
-    kv_c(0, 1).start()
+    kv_c(0).start()
 
     ones = jnp.ones((rows, hd), BF16)
 
@@ -153,8 +181,7 @@
 
         @pl.when(i == 0)
         def _():
-            kv_c(d, 0).wait_recv()
-            kv_c(d, 1).wait_recv()
+            kv_c(d).wait_recv()
 
         @pl.when(jnp.logical_and(d == 0, i > 0))
         def _():
@@ -162,19 +189,40 @@
 
         @pl.when(jnp.logical_and(d < 3, i == 1))
         def _():
-            kv_z(d + 1).wait_recv()
+            kv_z(d + 1, 0).wait_recv()
+            kv_z(d + 1, 1).wait_recv()
             kv_y(d + 1).start()
-            kv_c(d + 1, 0).start()
+
+        @pl.when(t == 1)
+        def _():
+            kv_z(3, 0).start()
+            kv_z(3, 1).start()
 
         @pl.when(jnp.logical_and(d < 3, i == 3))
         def _():
             kv_y(d + 1).wait_recv()
-            kv_c(d + 1, 1).start()
+            kv_c(d + 1).start()
+
+        @pl.when(t == 4)
+        def _():
+            for n in (1, 2, 3):
+                p_z(n).wait_recv()
+            p_x().start()
+
+        @pl.when(t == 8)
+        def _():
+            p_x().wait_recv()
+            p_y().start()
+
+        @pl.when(t == 12)
+        def _():
+            p_y().wait_recv()
+            p_c().start()
 
         me = at(zq, y, c)
         kinds, bases = [], []
         for k in range(4):
-            delta = (me - (zk * 4 + k) + blocks) % blocks
+            delta = (me - at(zk, k % 2, k // 2) + blocks) % blocks
             middle = blocks // 2
             kind = jnp.where(
                 delta == 0, 0, jnp.where(delta < middle, 1, jnp.where(delta == middle, 2, 3))
@@ -225,26 +273,42 @@
 
     lax.fori_loop(0, 16, step, 0)
 
+    p_c().wait_recv()
     obuf[x * ZS + z] = ost[z, x]
-    for d in range(4):
+    for d in (3, 2, 1, 0):
         o_copy(d, 1).wait_recv()
         if d:
             o_copy(d, 0).wait_recv()
-    mixed[...] = obuf[...]
-
+    total = None
+    for g in range(2):
+        mixed = jnp.concatenate([obuf[g * ZS + n] for n in range(ZS)], axis=1)
+        weights = jnp.concatenate(
+            [wobuf[n % 2, (n // 2) % 2, g, n // 4] for n in range(blocks)], axis=0
+        )
+        part = lax.dot_general(
+            mixed, weights, (((1,), (1,)), ((), ())), preferred_element_type=F32
+        )
+        total = part if total is None else total + part
+    out[...] = total.astype(BF16)
+
+    for part in range(3):
+        for d in (1, 2, 3):
+            w_z(part, d).wait_send()
+        w_y(part).wait_send()
+        w_c(part).wait_send()
     for d in range(4):
         if d:
-            w_z(d).wait_send()
-            kv_z(d).wait_send()
+            kv_z(d, 0).wait_send()
+            kv_z(d, 1).wait_send()
             q_z(d).wait_send()
+            p_z(d).wait_send()
             o_copy(d, 0).wait_send()
-        w_y(d).wait_send()
-        w_c(d, 0).wait_send()
-        w_c(d, 1).wait_send()
         kv_y(d).wait_send()
-        kv_c(d, 0).wait_send()
-        kv_c(d, 1).wait_send()
+        kv_c(d).wait_send()
         o_copy(d, 1).wait_send()
+    p_x().wait_send()
+    p_y().wait_send()
+    p_c().wait_send()
 
 
 def local_planes(frames, norm_gain, w_qkv, slopes, w_out):
@@ -254,17 +318,15 @@
     hd = w_qkv.shape[2] // heads
     total = heads * lax.axis_size("head")
     half = rows // 2
-    w_all = lax.all_gather(w_out, "tm", axis=1, tiled=True)
-    w_all = lax.all_gather(w_all, "head", axis=0, tiled=True)
     dma = pltpu.SemaphoreType.DMA
     vmem = pl.BlockSpec(memory_space=pltpu.VMEM)
-    mixed = pl.pallas_call(
+    return pl.pallas_call(
         kernel,
-        out_shape=jax.ShapeDtypeStruct((total, half, hd), BF16),
-        in_specs=[vmem, vmem, vmem, pl.BlockSpec(memory_space=pltpu.SMEM)],
+        out_shape=jax.ShapeDtypeStruct((half, width), BF16),
+        in_specs=[vmem, vmem, vmem, pl.BlockSpec(memory_space=pltpu.SMEM), vmem],
         out_specs=vmem,
         scratch_shapes=[
-            pltpu.VMEM((blocks,) + w_qkv.shape, BF16),
+            pltpu.VMEM((3, 2, 2, ZS) + w_qkv.shape[1:], BF16),
             pltpu.VMEM((blocks, 2, rows, hd), BF16),
             pltpu.VMEM((ZS, rows, hd), BF16),
             pltpu.VMEM((ZS, 2, rows, hd), BF16),
@@ -275,10 +337,11 @@
             pltpu.VMEM((4, rows, rows), F32),
             pltpu.VMEM((ZS * rows, 2 * hd), F32),
             pltpu.VMEM((ZS * rows, hd), F32),
+            pltpu.VMEM((2, 2, 2, ZS, w_out.shape[1], w_out.shape[0]), BF16),
         ] + [
-            dma((4,)), dma((4,)), dma((4,)), dma((4,)), dma((4, 2)), dma((4, 2)),
-            dma((4,)), dma((4,)), dma((4,)), dma((4,)), dma((4, 2)), dma((4, 2)),
-            dma((4,)), dma((4,)), dma((4, 2)), dma((4, 2)), dma((1,)),
+            dma((3, 4)), dma((3, 4)), dma((3,)), dma((3,)), dma((3,)), dma((3,)),
+            dma((4, 2)), dma((4, 2)), dma((4,)), dma((4,)), dma((4,)), dma((4,)),
+            dma((4,)), dma((4,)), dma((4, 2)), dma((4, 2)), dma((7,)), dma((7,)),
         ],
         compiler_params=pltpu.CompilerParams(
             collective_id=0, has_side_effects=True, vmem_limit_bytes=56 * 1024 * 1024
@@ -286,9 +349,7 @@
         cost_estimate=pl.CostEstimate(
             flops=11 * 10 ** 9, bytes_accessed=6 * 10 ** 6, transcendentals=17 * 10 ** 6
         ),
-    )(frames, norm_gain.reshape(1, -1), w_qkv, slopes)
-    flat = jnp.transpose(mixed, (1, 0, 2)).reshape(half, total * hd)
-    return jnp.dot(flat, w_all, preferred_element_type=F32).astype(BF16)
+    )(frames, norm_gain.reshape(1, -1), w_qkv, slopes, w_out.T)
 
 
 def local(frames, norm_gain, w_qkv, slopes, w_out):

time: 170 us -> 115 us (0.68)
  waiting for transfers between devices: 43.6 us -> 0 us
  between operations: 13.4 us -> 0.01 us
  Pallas kernels: 109 us -> 113 us
  matrix products: 3.14 us -> 0 us
    all_gather x2 -> x0, waiting for transfers between devices: 42.9 us -> none  [the longest x1 42.9 us: local_planes(): w_all = lax.all_gather(w_out, 'tm', axis=1, tiled=True)]
    pallas_call x1, Pallas kernels: 109 us -> 113 us  [local_planes(): pl.pallas_call(kernel, out_shape=jax.ShapeDtypeStruct((half, width), BF16...]
    dot_general x1 -> x0, matrix products: 3.14 us -> none  [local_planes(): return jnp.dot(flat, w_all, preferred_element_type=F32).astype(BF16)]
    unnamed x0 -> x1, local copies, waits for them, and re-layouts: none -> 1.87 us
  transfers between devices with their start and end apart: 2 -> 0, of which waited for: 1 -> 0; matrix products, arithmetic and copies ran while one was open for 1% -> 0% of each run, Pallas kernels for 64% -> 0%
where the time goes in v2:
time: 115 us; the launch traced here: 114 us
  Pallas kernels  113 us (98%)
  local copies, waits for them, and re-layouts  1.87 us (2%)
    pallas_call x1, Pallas kernels, local_planes(): pl.pallas_call(kernel, out_shape=jax.ShapeDtypeStruct((half, width), BF16...  113 us

profile of v2, /device:TPU:0, one launch (start us, length us, event | category | flops | bytes accessed | tf_op | source)
XLA Modules:
  0.0 114.4 jit_solution(16454866200278208182)
XLA Ops:
  0.0 112.5 %shard_map.55 = bf16[256,1024]{1,0:T(8,128)(2,1)} custom-call(bf16[512,1024]{1,0:T(8,128)(2,1)} %frames.1, f32[1,1024]{1,0:T(1,128)} %bitcast.3, bf16[3,64,512]{2,1,0:T(8,128)(2,1)} %w.1, f32[4]{0:T(128)} %slopes.1, bf16[64,512]{1,0:T(8,128)(2,1)} %bitcast.2), custom_call_target="tpu_custom_call" | custom-call | flops 11000000512 | bytes 6000000 | tf_op jit(solution)/shard_map/pallas_call | solution.py:323
  112.5 1.9 %copy.7 = bf16[256,1024]{1,0:T(8,128)(2,1)} copy(bf16[256,1024]{1,0:T(8,128)(2,1)} %shard_map.55) | data formatting | bytes 1048576

commit v3 on v2

--- a/solution.py
+++ b/solution.py
@@ -66,13 +66,13 @@
         dst = kvbuf.at[slot(z, y, c), j]
         return send(kvs.at[t, j], dst, kz_s.at[d, j], kz_r.at[d, j], to(at(t, y, c)))
 
-    def kv_y(d):
-        ref = kvbuf.at[slot(flip(z, d), y, c)]
-        return send(ref, ref, ky_s.at[d], ky_r.at[d], to(y_peer))
-
-    def kv_c(d):
-        ref = kvbuf.at[pl.ds(slot(flip(z, d), 0, c), 2)]
-        return send(ref, ref, kc_s.at[d], kc_r.at[d], to(c_peer))
+    def kv_y(d, j):
+        ref = kvbuf.at[slot(flip(z, d), y, c), j]
+        return send(ref, ref, ky_s.at[d, j], ky_r.at[d, j], to(y_peer))
+
+    def kv_c(d, j):
+        ref = kvbuf.at[pl.ds(slot(flip(z, d), 0, c), 2), j]
+        return send(ref, ref, kc_s.at[d, j], kc_r.at[d, j], to(c_peer))
 
     def q_z(d):
         t = flip(z, d)
@@ -108,7 +108,7 @@
         pl.semaphore_signal(barrier, inc=1, device_id=dev, device_id_type=MESH)
     pl.semaphore_wait(barrier, len(partners))
 
-    for part in range(3):
+    for part in (0, 1):
         for d in (1, 2, 3):
             w_z(part, d).start()
     for part in range(3):
@@ -139,6 +139,8 @@
         return jnp.dot(normed[...], weights, preferred_element_type=F32)
 
     z_arrived(0)
+    for d in (1, 2, 3):
+        w_z(2, d).start()
     ii = lax.broadcasted_iota(jnp.int32, (rows, rows), 0)
     jj = lax.broadcasted_iota(jnp.int32, (rows, rows), 1)
     lin = (ii - jj).astype(F32) * slope
@@ -157,19 +159,26 @@
     for d in (1, 2, 3):
         q_z(d).start()
     qbuf[z] = qs[z]
+    mine = slot(z, y, c)
     for part in (1, 2):
         y_arrived(part)
-        res = project(part).astype(BF16)
+        res = project(part)
         for h in range(ZS):
-            kvs[h, part - 1] = res[:, h * hd:(h + 1) * hd]
+            piece = res[:, h * hd:(h + 1) * hd]
+            if part == 1:
+                for a in range(0, rows, hd):
+                    kvs[h, 0, a:a + hd, :] = piece[a:a + hd, :].T.astype(BF16)
+            else:
+                kvs[h, 1] = piece.astype(BF16)
         for d in (1, 2):
             kv_z(d, part - 1).start()
-    kvbuf[slot(z, y, c)] = kvs[z]
-    kv_y(0).start()
+        kvbuf[mine, part - 1] = kvs[z, part - 1]
+        kv_y(0, part - 1).start()
     for d in (1, 2, 3):
         p_z(d).start()
-    kv_y(0).wait_recv()
-    kv_c(0).start()
+    for j in range(2):
+        kv_y(0, j).wait_recv()
+        kv_c(0, j).start()
 
     ones = jnp.ones((rows, hd), BF16)
 
@@ -181,7 +190,8 @@
 
         @pl.when(i == 0)
         def _():
-            kv_c(d).wait_recv()
+            kv_c(d, 0).wait_recv()
+            kv_c(d, 1).wait_recv()
 
         @pl.when(jnp.logical_and(d == 0, i > 0))
         def _():
@@ -189,9 +199,9 @@
 
         @pl.when(jnp.logical_and(d < 3, i == 1))
         def _():
-            kv_z(d + 1, 0).wait_recv()
-            kv_z(d + 1, 1).wait_recv()
-            kv_y(d + 1).start()
+            for j in range(2):
+                kv_z(d + 1, j).wait_recv()
+                kv_y(d + 1, j).start()
 
         @pl.when(t == 1)
         def _():
@@ -200,8 +210,9 @@
 
         @pl.when(jnp.logical_and(d < 3, i == 3))
         def _():
-            kv_y(d + 1).wait_recv()
-            kv_c(d + 1).start()
+            for j in range(2):
+                kv_y(d + 1, j).wait_recv()
+                kv_c(d + 1, j).start()
 
         @pl.when(t == 4)
         def _():
@@ -230,32 +241,44 @@
             kinds.append(kind)
             far = jnp.where(delta <= middle, delta, blocks - delta) * rows
             bases.append(-slope * far.astype(F32))
-        for r in (0, half):
-            q = qbuf[zq, r:r + half, :]
+        def score(r, k):
+            keys = kvbuf[zk * 4 + k, 0]
+            keys = jnp.concatenate([keys[a:a + hd] for a in range(0, rows, hd)], axis=1)
+            s = jnp.dot(qbuf[zq, r:r + half, :], keys, preferred_element_type=F32)
+            s = s + tiles[kinds[k], r:r + half, :]
+            m = s[:, :hd]
+            for a in range(hd, rows, hd):
+                m = jnp.maximum(m, s[:, a:a + hd])
+            return s, m + bases[k]
+
+        def begin(r, tops):
             place = pl.ds(pl.multiple_of(zq * rows + r, half), half)
-            raw, top = [], None
-            for k in range(4):
-                s = lax.dot_general(
-                    q, kvbuf[zk * 4 + k, 0], (((1,), (1,)), ((), ())), preferred_element_type=F32
-                )
-                s = s + tiles[kinds[k], r:r + half, :]
-                raw.append(s)
-                m = s[:, :hd]
-                for a in range(hd, rows, hd):
-                    m = jnp.maximum(m, s[:, a:a + hd])
-                m = m + bases[k]
-                top = m if top is None else jnp.maximum(top, m)
+            top = jnp.maximum(jnp.maximum(tops[0], tops[1]), jnp.maximum(tops[2], tops[3]))
             old = peak[place, :]
             new = jnp.maximum(old, jnp.max(top, axis=-1, keepdims=True))
             peak[place, :] = new
             shrink = jnp.exp2(old - new)
-            col = new[:, :1]
-            total = acc[place, :] * jnp.concatenate([shrink, shrink], axis=1)
-            for k in range(4):
-                p = jnp.exp2(raw[k] - (col - bases[k])).astype(BF16)
-                v = jnp.concatenate([kvbuf[zk * 4 + k, 1], ones], axis=1)
-                total = total + jnp.dot(p, v, preferred_element_type=F32)
-            acc[place, :] = total
+            return new[:, :1], acc[place, :] * jnp.concatenate([shrink, shrink], axis=1)
+
+        def add(total, s, col, k):
+            p = jnp.exp2(s - (col - bases[k])).astype(BF16)
+            v = jnp.concatenate([kvbuf[zk * 4 + k, 1], ones], axis=1)
+            return total + jnp.dot(p, v, preferred_element_type=F32)
+
+        def finish(r, total):
+            acc[pl.ds(pl.multiple_of(zq * rows + r, half), half), :] = total
+
+        first = [score(0, k) for k in range(4)]
+        col, total = begin(0, [m for _, m in first])
+        second = []
+        for k in range(4):
+            second.append(score(half, k))
+            total = add(total, first[k][0], col, k)
+        finish(0, total)
+        col, total = begin(half, [m for _, m in second])
+        for k in range(4):
+            total = add(total, second[k][0], col, k)
+        finish(half, total)
 
         @pl.when(d == 3)
         def _():
@@ -303,8 +326,9 @@
             q_z(d).wait_send()
             p_z(d).wait_send()
             o_copy(d, 0).wait_send()
-        kv_y(d).wait_send()
-        kv_c(d).wait_send()
+        for j in range(2):
+            kv_y(d, j).wait_send()
+            kv_c(d, j).wait_send()
         o_copy(d, 1).wait_send()
     p_x().wait_send()
     p_y().wait_send()
@@ -340,7 +364,7 @@
             pltpu.VMEM((2, 2, 2, ZS, w_out.shape[1], w_out.shape[0]), BF16),
         ] + [
             dma((3, 4)), dma((3, 4)), dma((3,)), dma((3,)), dma((3,)), dma((3,)),
-            dma((4, 2)), dma((4, 2)), dma((4,)), dma((4,)), dma((4,)), dma((4,)),
+            dma((4, 2)), dma((4, 2)), dma((4, 2)), dma((4, 2)), dma((4, 2)), dma((4, 2)),
             dma((4,)), dma((4,)), dma((4, 2)), dma((4, 2)), dma((7,)), dma((7,)),
         ],
         compiler_params=pltpu.CompilerParams(

time: 115 us -> 114 us (level)
  no operation moved by 1% of the time
where the time goes in v3:
time: 114 us; the launch traced here: 113 us
  Pallas kernels  112 us (98%)
  local copies, waits for them, and re-layouts  1.87 us (2%)
    pallas_call x1, Pallas kernels, local_planes(): pl.pallas_call(kernel, out_shape=jax.ShapeDtypeStruct((half, width), BF16...  112 us

profile of v3, /device:TPU:0, one launch (start us, length us, event | category | flops | bytes accessed | tf_op | source)
XLA Modules:
  0.0 113.4 jit_solution(18148590044900454579)
XLA Ops:
  0.0 111.6 %shard_map.55 = bf16[256,1024]{1,0:T(8,128)(2,1)} custom-call(bf16[512,1024]{1,0:T(8,128)(2,1)} %frames.1, f32[1,1024]{1,0:T(1,128)} %bitcast.3, bf16[3,64,512]{2,1,0:T(8,128)(2,1)} %w.1, f32[4]{0:T(128)} %slopes.1, bf16[64,512]{1,0:T(8,128)(2,1)} %bitcast.2), custom_call_target="tpu_custom_call" | custom-call | flops 11000000512 | bytes 6000000 | tf_op jit(solution)/shard_map/pallas_call | solution.py:347
  111.6 1.9 %copy.7 = bf16[256,1024]{1,0:T(8,128)(2,1)} copy(bf16[256,1024]{1,0:T(8,128)(2,1)} %shard_map.55) | data formatting | bytes 1048576

commit v4 on v3

--- a/solution.py
+++ b/solution.py
@@ -49,9 +49,18 @@
             src_ref=src, dst_ref=dst, send_sem=ss, recv_sem=rs, device_id=dev, device_id_type=MESH
         )
 
+    inner = jnp.logical_or(z == 1, z == 2)
+    outer = jnp.logical_or(z == 0, z == 3)
+
     def w_z(part, d):
-        dev = to(at(flip(z, d), y, c))
-        return send(w.at[part], wbuf.at[part, c, y, z], wz_s.at[part, d], wz_r.at[part, d], dev)
+        if d == 0:
+            src, dst, t = w.at[part], wbuf.at[part, c, y, z], flip(z, 1)
+        else:
+            near = z // 2
+            src = wbuf.at[part, c, y, pl.ds(2 * (near if d == 1 else 1 - near), 2)]
+            dst, t = src, (3 - z if d == 1 else flip(z, 1))
+        dev = to(at(t, y, c))
+        return send(src, dst, wz_s.at[part, d], wz_r.at[part, d], dev)
 
     def w_y(part):
         ref = wbuf.at[part, c, y]
@@ -108,23 +117,32 @@
         pl.semaphore_signal(barrier, inc=1, device_id=dev, device_id_type=MESH)
     pl.semaphore_wait(barrier, len(partners))
 
-    for part in (0, 1):
-        for d in (1, 2, 3):
-            w_z(part, d).start()
+    for part in range(3):
+        w_z(part, 0).start()
     for part in range(3):
         wbuf[part, c, y, z] = w[part]
     wobuf[c, y, x, z] = w_out[...]
 
-    wide = frames[...].astype(F32)
-    inverse_root = lax.rsqrt(jnp.mean(wide * wide, axis=-1, keepdims=True) + 1e-06)
-    normed[...] = (wide * inverse_root * gain[...]).astype(BF16)
-
     log2e = math.log2(math.e)
     slope = slopes[z] * log2e
 
+    def z_near(part):
+        w_z(part, 0).wait_recv()
+
+        @pl.when(inner)
+        def _():
+            w_z(part, 1).start()
+
     def z_arrived(part):
-        for d in (1, 2, 3):
-            w_z(part, d).wait_recv()
+        @pl.when(inner)
+        def _():
+            w_z(part, 1).wait_recv()
+            w_z(part, 2).start()
+
+        @pl.when(outer)
+        def _():
+            w_z(part, 2).wait_recv()
+
         w_y(part).start()
 
     def y_arrived(part):
@@ -138,9 +156,14 @@
         )
         return jnp.dot(normed[...], weights, preferred_element_type=F32)
 
+    z_near(0)
+    z_near(1)
+    z_near(2)
+    wide = frames[...].astype(F32)
+    inverse_root = lax.rsqrt(jnp.mean(wide * wide, axis=-1, keepdims=True) + 1e-06)
+    normed[...] = (wide * inverse_root * gain[...]).astype(BF16)
+
     z_arrived(0)
-    for d in (1, 2, 3):
-        w_z(2, d).start()
     ii = lax.broadcasted_iota(jnp.int32, (rows, rows), 0)
     jj = lax.broadcasted_iota(jnp.int32, (rows, rows), 1)
     lin = (ii - jj).astype(F32) * slope
@@ -153,10 +176,12 @@
     z_arrived(1)
     y_arrived(0)
     z_arrived(2)
+    for d in (2, 3, 1):
+        p_z(d).start()
     res = (project(0) * (hd ** -0.5 * log2e)).astype(BF16)
     for h in range(ZS):
         qs[h] = res[:, h * hd:(h + 1) * hd]
-    for d in (1, 2, 3):
+    for d in (2, 3, 1):
         q_z(d).start()
     qbuf[z] = qs[z]
     mine = slot(z, y, c)
@@ -170,15 +195,15 @@
                     kvs[h, 0, a:a + hd, :] = piece[a:a + hd, :].T.astype(BF16)
             else:
                 kvs[h, 1] = piece.astype(BF16)
-        for d in (1, 2):
+        for d in (2, 1):
             kv_z(d, part - 1).start()
         kvbuf[mine, part - 1] = kvs[z, part - 1]
         kv_y(0, part - 1).start()
-    for d in (1, 2, 3):
-        p_z(d).start()
     for j in range(2):
         kv_y(0, j).wait_recv()
         kv_c(0, j).start()
+    kv_z(2, 0).wait_send()
+    kv_z(3, 0).start()
 
     ones = jnp.ones((rows, hd), BF16)
 
@@ -205,7 +230,7 @@
 
         @pl.when(t == 1)
         def _():
-            kv_z(3, 0).start()
+            kv_z(2, 1).wait_send()
             kv_z(3, 1).start()
 
         @pl.when(jnp.logical_and(d < 3, i == 3))
@@ -315,14 +340,20 @@
     out[...] = total.astype(BF16)
 
     for part in range(3):
-        for d in (1, 2, 3):
-            w_z(part, d).wait_send()
+        w_z(part, 0).wait_send()
+
+        @pl.when(inner)
+        def _():
+            w_z(part, 1).wait_send()
+            w_z(part, 2).wait_send()
+
         w_y(part).wait_send()
         w_c(part).wait_send()
     for d in range(4):
         if d:
-            kv_z(d, 0).wait_send()
-            kv_z(d, 1).wait_send()
+            if d != 2:
+                kv_z(d, 0).wait_send()
+                kv_z(d, 1).wait_send()
             q_z(d).wait_send()
             p_z(d).wait_send()
             o_copy(d, 0).wait_send()

time: 114 us -> 114 us (level)
  no operation moved by 1% of the time
where the time goes in v4:
time: 114 us; the launch traced here: 113 us
  Pallas kernels  112 us (98%)
  local copies, waits for them, and re-layouts  1.87 us (2%)
    pallas_call x1, Pallas kernels, local_planes(): pl.pallas_call(kernel, out_shape=jax.ShapeDtypeStruct((half, width), BF16...  112 us

profile of v4, /device:TPU:0, one launch (start us, length us, event | category | flops | bytes accessed | tf_op | source)
XLA Modules:
  0.0 113.4 jit_solution(9685868434634898017)
XLA Ops:
  0.0 111.5 %shard_map.55 = bf16[256,1024]{1,0:T(8,128)(2,1)} custom-call(bf16[512,1024]{1,0:T(8,128)(2,1)} %frames.1, f32[1,1024]{1,0:T(1,128)} %bitcast.3, bf16[3,64,512]{2,1,0:T(8,128)(2,1)} %w.1, f32[4]{0:T(128)} %slopes.1, bf16[64,512]{1,0:T(8,128)(2,1)} %bitcast.2), custom_call_target="tpu_custom_call" | custom-call | flops 11000000512 | bytes 6000000 | tf_op jit(solution)/shard_map/pallas_call | solution.py:378
  111.5 1.9 %copy.7 = bf16[256,1024]{1,0:T(8,128)(2,1)} copy(bf16[256,1024]{1,0:T(8,128)(2,1)} %shard_map.55) | data formatting | bytes 1048576

commit v5 on v4

--- a/solution.py
+++ b/solution.py
@@ -207,119 +207,124 @@
 
     ones = jnp.ones((rows, hd), BF16)
 
+    wide_rows = 2 * rows
+
     def step(t, carry):
-        d, i = t // 4, t % 4
+        d, i = t // 2, t % 2
         zk = flip(z, d)
-        e = jnp.where(d == 3, 3 - i, i)
-        zq = flip(z, e)
+        g = jnp.where(d == 3, 1 - i, i)
+        first = 2 * ((z // 2 + g) % 2)
+        place = pl.ds(pl.multiple_of(first * rows, wide_rows), wide_rows)
+
+        @pl.when(t == 0)
+        def _():
+            q_z(1).wait_recv()
+            kv_z(2, 1).wait_send()
+            kv_z(3, 1).start()
+
+        @pl.when(t == 1)
+        def _():
+            q_z(2).wait_recv()
+            q_z(3).wait_recv()
 
         @pl.when(i == 0)
         def _():
             kv_c(d, 0).wait_recv()
             kv_c(d, 1).wait_recv()
 
-        @pl.when(jnp.logical_and(d == 0, i > 0))
-        def _():
-            q_z(i).wait_recv()
-
-        @pl.when(jnp.logical_and(d < 3, i == 1))
+        @pl.when(jnp.logical_and(d < 3, i == 0))
         def _():
             for j in range(2):
                 kv_z(d + 1, j).wait_recv()
                 kv_y(d + 1, j).start()
 
-        @pl.when(t == 1)
-        def _():
-            kv_z(2, 1).wait_send()
-            kv_z(3, 1).start()
-
-        @pl.when(jnp.logical_and(d < 3, i == 3))
+        @pl.when(jnp.logical_and(d < 3, i == 1))
         def _():
             for j in range(2):
                 kv_y(d + 1, j).wait_recv()
                 kv_c(d + 1, j).start()
 
-        @pl.when(t == 4)
+        @pl.when(t == 2)
         def _():
             for n in (1, 2, 3):
                 p_z(n).wait_recv()
             p_x().start()
 
-        @pl.when(t == 8)
+        @pl.when(t == 4)
         def _():
             p_x().wait_recv()
             p_y().start()
 
-        @pl.when(t == 12)
+        @pl.when(t == 6)
         def _():
             p_y().wait_recv()
             p_c().start()
 
-        me = at(zq, y, c)
-        kinds, bases = [], []
-        for k in range(4):
-            delta = (me - at(zk, k % 2, k // 2) + blocks) % blocks
+        def offset(n, k):
+            delta = (at(first + n, y, c) - at(zk, k % 2, k // 2) + blocks) % blocks
             middle = blocks // 2
             kind = jnp.where(
                 delta == 0, 0, jnp.where(delta < middle, 1, jnp.where(delta == middle, 2, 3))
             )
-            kinds.append(kind)
             far = jnp.where(delta <= middle, delta, blocks - delta) * rows
-            bases.append(-slope * far.astype(F32))
-        def score(r, k):
+            return kind, -slope * far.astype(F32)
+
+        offsets = [[offset(n, k) for k in range(4)] for n in range(2)]
+        query = qbuf[pl.ds(first, 2)].reshape(wide_rows, hd)
+        scores, tops = [], [None, None]
+        for k in range(4):
             keys = kvbuf[zk * 4 + k, 0]
             keys = jnp.concatenate([keys[a:a + hd] for a in range(0, rows, hd)], axis=1)
-            s = jnp.dot(qbuf[zq, r:r + half, :], keys, preferred_element_type=F32)
-            s = s + tiles[kinds[k], r:r + half, :]
-            m = s[:, :hd]
-            for a in range(hd, rows, hd):
-                m = jnp.maximum(m, s[:, a:a + hd])
-            return s, m + bases[k]
-
-        def begin(r, tops):
-            place = pl.ds(pl.multiple_of(zq * rows + r, half), half)
-            top = jnp.maximum(jnp.maximum(tops[0], tops[1]), jnp.maximum(tops[2], tops[3]))
-            old = peak[place, :]
-            new = jnp.maximum(old, jnp.max(top, axis=-1, keepdims=True))
-            peak[place, :] = new
-            shrink = jnp.exp2(old - new)
-            return new[:, :1], acc[place, :] * jnp.concatenate([shrink, shrink], axis=1)
-
-        def add(total, s, col, k):
-            p = jnp.exp2(s - (col - bases[k])).astype(BF16)
+            both = jnp.dot(query, keys, preferred_element_type=F32)
+            parts = []
+            for n in range(2):
+                kind, base = offsets[n][k]
+                s = both[n * rows:(n + 1) * rows] + tiles[kind]
+                parts.append(s)
+                m = s[:, :hd]
+                for a in range(hd, rows, hd):
+                    m = jnp.maximum(m, s[:, a:a + hd])
+                m = m + base
+                tops[n] = m if k == 0 else jnp.maximum(tops[n], m)
+            scores.append(parts)
+        old = peak[place, :]
+        top = jnp.concatenate([jnp.max(m, axis=-1, keepdims=True) for m in tops], axis=0)
+        new = jnp.maximum(old, top)
+        peak[place, :] = new
+        shrink = jnp.exp2(old - new)
+        total = acc[place, :] * jnp.concatenate([shrink, shrink], axis=1)
+        cols = [new[:rows, :1], new[rows:, :1]]
+        for k in range(4):
+            p = [jnp.exp2(scores[k][n] - (cols[n] - offsets[n][k][1])).astype(BF16) for n in range(2)]
             v = jnp.concatenate([kvbuf[zk * 4 + k, 1], ones], axis=1)
-            return total + jnp.dot(p, v, preferred_element_type=F32)
-
-        def finish(r, total):
-            acc[pl.ds(pl.multiple_of(zq * rows + r, half), half), :] = total
-
-        first = [score(0, k) for k in range(4)]
-        col, total = begin(0, [m for _, m in first])
-        second = []
-        for k in range(4):
-            second.append(score(half, k))
-            total = add(total, first[k][0], col, k)
-        finish(0, total)
-        col, total = begin(half, [m for _, m in second])
-        for k in range(4):
-            total = add(total, second[k][0], col, k)
-        finish(half, total)
+            total = total + jnp.dot(
+                jnp.concatenate(p, axis=0), v, preferred_element_type=F32
+            )
+        acc[place, :] = total
 
         @pl.when(d == 3)
         def _():
-            for s in range(2):
-                place = pl.ds(pl.multiple_of(zq * rows + s * half, half), half)
-                val = acc[place, :]
-                ost[zq, s] = (val[:, :hd] / val[:, hd:]).astype(BF16)
-            o_copy(e, 1).start()
-
-        @pl.when(jnp.logical_and(d == 3, e > 0))
-        def _():
-            o_copy(e, 0).start()
+            for n in range(2):
+                for s in range(2):
+                    start = pl.multiple_of((first + n) * rows + s * half, half)
+                    val = acc[pl.ds(start, half), :]
+                    ost[first + n, s] = (val[:, :hd] / val[:, hd:]).astype(BF16)
+
+        @pl.when(jnp.logical_and(d == 3, g == 1))
+        def _():
+            for e in (2, 3):
+                o_copy(e, 0).start()
+                o_copy(e, 1).start()
+
+        @pl.when(jnp.logical_and(d == 3, g == 0))
+        def _():
+            o_copy(1, 0).start()
+            o_copy(1, 1).start()
+            o_copy(0, 1).start()
 
         return carry
 
-    lax.fori_loop(0, 16, step, 0)
+    lax.fori_loop(0, 8, step, 0)
 
     p_c().wait_recv()
     obuf[x * ZS + z] = ost[z, x]

time: 114 us -> 117 us (1.026)
  Pallas kernels: 112 us -> 115 us
    pallas_call x1, Pallas kernels: 112 us -> 115 us  [local_planes(): pl.pallas_call(kernel, out_shape=jax.ShapeDtypeStruct((half, width), BF16...]
where the time goes in v5:
time: 117 us
  Pallas kernels  115 us (98%)
  local copies, waits for them, and re-layouts  1.87 us (2%)
    pallas_call x1, Pallas kernels, local_planes(): pl.pallas_call(kernel, out_shape=jax.ShapeDtypeStruct((half, width), BF16...  115 us

profile of v5, /device:TPU:0, one launch (start us, length us, event | category | flops | bytes accessed | tf_op | source)
XLA Modules:
  0.0 116.9 jit_solution(3549070348491120266)
XLA Ops:
  0.0 115.0 %shard_map.55 = bf16[256,1024]{1,0:T(8,128)(2,1)} custom-call(bf16[512,1024]{1,0:T(8,128)(2,1)} %frames.1, f32[1,1024]{1,0:T(1,128)} %bitcast.3, bf16[3,64,512]{2,1,0:T(8,128)(2,1)} %w.1, f32[4]{0:T(128)} %slopes.1, bf16[64,512]{1,0:T(8,128)(2,1)} %bitcast.2), custom_call_target="tpu_custom_call" | custom-call | flops 11000000512 | bytes 6000000 | tf_op jit(solution)/shard_map/pallas_call | solution.py:383
  115.0 1.9 %copy.7 = bf16[256,1024]{1,0:T(8,128)(2,1)} copy(bf16[256,1024]{1,0:T(8,128)(2,1)} %shard_map.55) | data formatting | bytes 1048576

commit v6 on v3

--- a/solution.py
+++ b/solution.py
@@ -261,7 +261,7 @@
             return new[:, :1], acc[place, :] * jnp.concatenate([shrink, shrink], axis=1)
 
         def add(total, s, col, k):
-            p = jnp.exp2(s - (col - bases[k])).astype(BF16)
+            p = jnp.exp2((s - (col - bases[k])).astype(BF16))
             v = jnp.concatenate([kvbuf[zk * 4 + k, 1], ones], axis=1)
             return total + jnp.dot(p, v, preferred_element_type=F32)
 

time: 114 us -> 113 us (level)
  no operation moved by 1% of the time
where the time goes in v6:
time: 113 us
  Pallas kernels  111 us (98%)
  local copies, waits for them, and re-layouts  1.87 us (2%)
    pallas_call x1, Pallas kernels, local_planes(): pl.pallas_call(kernel, out_shape=jax.ShapeDtypeStruct((half, width), BF16...  111 us

profile of v6, /device:TPU:0, one launch (start us, length us, event | category | flops | bytes accessed | tf_op | source)
XLA Modules:
  0.0 112.8 jit_solution(15077872927361608375)
XLA Ops:
  0.0 110.9 %shard_map.55 = bf16[256,1024]{1,0:T(8,128)(2,1)} custom-call(bf16[512,1024]{1,0:T(8,128)(2,1)} %frames.1, f32[1,1024]{1,0:T(1,128)} %bitcast.3, bf16[3,64,512]{2,1,0:T(8,128)(2,1)} %w.1, f32[4]{0:T(128)} %slopes.1, bf16[64,512]{1,0:T(8,128)(2,1)} %bitcast.2), custom_call_target="tpu_custom_call" | custom-call | flops 11000000512 | bytes 6000000 | tf_op jit(solution)/shard_map/pallas_call | solution.py:347
  110.9 1.9 %copy.7 = bf16[256,1024]{1,0:T(8,128)(2,1)} copy(bf16[256,1024]{1,0:T(8,128)(2,1)} %shard_map.55) | data formatting | bytes 1048576
